TPU v7x, 256 devices: a whole 4x4x8 slice. The times are simulated.
256 devices in a mesh: aux: 8 (over z_lo, y), virt: 32 (over x, z_hi, core).
Axes of the slice: x: 4, y: 4, z: 8 (z_hi: 4, z_lo: 2; z = z_hi * 2 + z_lo), core: 2. Of those that a mesh axis runs over, the one named last changes fastest.
Arguments:
- df_blocks: bfloat16 [512, 1280, 1280], P('aux', 'virt'), may hold values from -1.25 to 1.25
- fno_rotation: bfloat16 [1280, 640], replicated, may hold values from -0.15625 to 0.15625
- tile_pairs: int32 [64, 2], P('virt'), may hold values from 0 to 639
Outputs:
- slab_tiles: float32 [640, 64, 640], P('aux', 'virt')
All inputs are finite; a program needn't handle non-finite values.
Results may differ from a plain program's by a relative error of at most 0.0057.
Values may be sent and summed in bfloat16 or wider, within the bound.
A program may use at most 64 MiB of HBM per device.

v0:
```python
import jax
import jax.numpy as jnp
from jax import lax
from jax.sharding import PartitionSpec as P


def local(df_blocks, fno_rotation, tile_pairs):
    natural = fno_rotation.shape[1]
    tile_count = tile_pairs.shape[0]
    halfway = jnp.einsum(
        "pab,bd->pda", df_blocks, fno_rotation, preferred_element_type=jnp.float32
    ).astype(jnp.bfloat16)
    fno_ints = jnp.einsum(
        "pda,ac->pdc",
        lax.all_to_all(halfway, "virt", split_axis=1, concat_axis=2, tiled=True),
        fno_rotation,
        preferred_element_type=jnp.float32,
    ).astype(jnp.bfloat16)
    pairs_all = lax.all_gather(tile_pairs, "virt", axis=0, tiled=True)
    groups = lax.axis_size("virt")
    wanted = jnp.transpose(pairs_all.reshape(groups, tile_count, 2), (0, 2, 1)).reshape(-1)
    picker = (wanted[:, None] == jnp.arange(natural, dtype=jnp.int32)[None, :]).astype(jnp.bfloat16)
    picked = jnp.einsum("pyc,rc->pry", fno_ints, picker, preferred_element_type=jnp.float32).astype(
        jnp.bfloat16
    )
    fetched = lax.all_to_all(picked, "virt", split_axis=1, concat_axis=2, tiled=True)
    left_rows = fetched[:, :tile_count]
    right_rows = fetched[:, tile_count:]
    return lax.psum_scatter(
        jnp.einsum("ptc,ptd->ctd", left_rows, right_rows, preferred_element_type=jnp.float32),
        "aux",
        scatter_dimension=0,
        tiled=True,
    )


def solution(mesh):
    placed = (P("aux", "virt", None), P(), P("virt", None))
    return jax.shard_map(
        local, mesh=mesh, in_specs=placed, out_specs=P("aux", "virt", None), check_vma=False
    )
```

profile of v0, /device:TPU:1, one launch (start us, length us, event | category | flops | bytes accessed | tf_op | source)
XLA Modules:
  0.0 312.1 jit_solution(15711129783196840575)
XLA Ops:
  6.5 0.0 copy-start
  6.5 1.4 copy-done
  8.0 9.6 %convert_bitcast_fusion = bf16[64,640,40]{1,0,2:T(8,128)(2,1)} fusion(bf16[64,40,1280]{2,1,0:T(8,128)(2,1)} %param.3, bf16[1280,640]{1,0:T(8,128)(2,1)S(1)} %copy-done), kind=kOutput, calls=%fused_computation.2 | convolution fusion | flops 4195942400 | bytes 11468800 | tf_op jit(solution)/shard_map/pab,bd->pda/dot_general | solution.py:10
  17.6 11.0 %copy.19 = bf16[64,640,40]{0,2,1:T(8,128)(2,1)} copy(bf16[64,640,40]{1,0,2:T(8,128)(2,1)} %convert_bitcast_fusion) | data formatting | bytes 6553600 | tf_op jit(solution)/shard_map/convert_element_type | solution.py:12
  28.6 8.6 %reshape.11 = bf16[32,2,25600]{2,1,0:T(2,128)(2,1)} reshape(bf16[640,40,64]{2,1,0:T(8,128)(2,1)} %bitcast.37) | data formatting | bytes 6553600
  37.2 0.0 copy-start.1
  37.2 12.8 %all-to-all-start = ((bf16[32,2,25600]{2,1,0:T(2,128)(2,1)}), bf16[32,2,25600]{2,1,0:T(2,128)(2,1)}, u32[]{:S(2)}, u32[]{:S(2)}) async-start(bf16[32,2,25600]{2,1,0:T(2,128)(2,1)} %reshape.11), calls=%async_computation | async-start | bytes 6553600 | tf_op jit(solution)/shard_map/all_to_all | solution.py:15
  50.0 0.0 all-reduce.3.cloned.1.call-start
  50.1 0.0 copy-done.1
  50.1 109.7 %all-gather = s32[32,2,2]{2,1,0:T(2,128)S(1)} all-gather(s32[1,2,2]{2,1,0:T(2,128)S(1)} %bitcast.44), channel_id=1, replica_groups=mesh['aux'=8,'virt'=32] {'virt'}, dimensions={0}, use_global_device_ids=true | all-gather | bytes 528 | tf_op jit(solution)/shard_map/all_gather | solution.py:19
  159.8 0.3 copy.17
  160.1 0.1 eq.15
  160.3 0.0 all-to-all-done
  160.3 8.7 %reshape.12 = bf16[640,40,64]{2,1,0:T(8,128)(2,1)} reshape(bf16[32,2,25600]{2,1,0:T(2,128)(2,1)} %all-to-all-done) | data formatting | bytes 6553600
  169.0 7.3 %copy.20 = bf16[64,20,32,40]{0,3,2,1:T(8,128)(2,1)} copy(bf16[64,20,32,40]{0,3,1,2:T(8,128)(2,1)} %bitcast.38) | data formatting | bytes 6553600 | tf_op jit(solution)/shard_map/all_to_all | solution.py:15
  176.3 6.4 %fusion.12 = bf16[64,128,20]{1,0,2:T(8,128)(2,1)S(1)} fusion(bf16[64,20,1280]{0,2,1:T(8,128)(2,1)} %bitcast.36, bf16[1280,640]{1,0:T(8,128)(2,1)S(1)} %copy-done, s32[128]{0:T(128)S(1)} %eq.15), kind=kOutput, calls=%fused_computation.9 | convolution fusion | flops 2307932160 | bytes 5243392 | tf_op jit(solution)/shard_map/pyc,rc->pry/dot_general | solution.py:23
  182.7 0.4 copy.22
  183.1 0.4 reshape.13
  183.6 17.7 %all_to_all.36 = bf16[32,2,2560]{2,1,0:T(2,128)(2,1)S(1)} all-to-all(bf16[32,2,2560]{2,1,0:T(2,128)(2,1)S(1)} %reshape.13), channel_id=1, replica_groups=mesh['aux'=8,'virt'=32] {'virt'}, dimensions={0} | all-to-all | bytes 655360 | tf_op jit(solution)/shard_map/all_to_all | solution.py:26
  201.3 0.6 reshape.14
  201.9 0.1 copy.23
  202.0 0.2 copy.24
  202.3 0.5 fusion.20
  202.7 2.3 convolution_bitcast_fusion
  205.0 7.3 %copy.27 = f32[640,2,640]{2,1,0:T(2,128)} copy(f32[640,2,640]{0,2,1:T(8,128)} %convolution_bitcast_fusion) | data formatting | bytes 6553600 | tf_op jit(solution)/shard_map/ptc,ptd->ctd/transpose | solution.py:30
  212.4 0.0 copy-start.2
  212.4 0.0 all-reduce.3.cloned.1.call-update
  212.4 0.6 copy-done.2
  213.0 0.6 dynamic-slice
  214.3 89.1 %all-reduce.3.cloned.1.call-done = f32[640,2,640]{2,1,0:T(2,128)} async-done(((f32[640,2,640]{2,1,0:T(2,128)}), f32[640,2,640]{2,1,0:T(2,128)}) %all-reduce.3.cloned.1.call-update) | async-done | bytes 3276816
  303.4 1.8 constant_dynamic-slice_fusion
Async XLA Ops:
  6.5 1.4 copy-start
  37.2 12.8 %copy-start.1 = (s32[2,2]{1,0:T(2,128)S(1)}, s32[2,2]{1,0:T(2,128)}, u32[]{:S(2)}) copy-start(s32[2,2]{1,0:T(2,128)} %param.5) | copy-start | bytes 52
  37.2 123.0 %all-to-all-start = ((bf16[32,2,25600]{2,1,0:T(2,128)(2,1)}), bf16[32,2,25600]{2,1,0:T(2,128)(2,1)}, u32[]{:S(2)}, u32[]{:S(2)}) async-start(bf16[32,2,25600]{2,1,0:T(2,128)(2,1)} %reshape.11), calls=%async_computation | async-start | bytes 6553600 | tf_op jit(solution)/shard_map/all_to_all | solution.py:15
  50.0 253.4 %all-reduce.3.cloned.1.call-start = ((), (), s32[]{:S(2)}) async-start(), calls=%async_computation.2 | async-start | bytes 6553600
  212.4 0.7 copy-start.2
Sparse Core Ops, SparseCore 0:
  212.5 90.8 all-reduce.2
where the time goes:
time: 313 us; the launch traced here: 312 us
  blocking collectives  127 us (41%)
  waiting for transfers between devices  89.2 us (28%)
  local copies, waits for them, and re-layouts  50.2 us (16%)
  matrix products  18.3 us (6%)
  between operations  14.1 us (5%)
  starting transfers between devices  12.8 us (4%)
    all_gather x1, blocking collectives, local(): pairs_all = lax.all_gather(tile_pairs, 'virt', axis=0, tiled=True)  110 us
    unnamed x2, waiting for transfers between devices  89.2 us
    unnamed x12, local copies, waits for them, and re-layouts  22.8 us
    all_to_all x1, blocking collectives, local(): lax.all_to_all(picked, 'virt', split_axis=1, concat_axis=2, tiled=True)  17.7 us
    all_to_all x1, starting transfers between devices, local(): lax.all_to_all(halfway, 'virt', split_axis=1, concat_axis=2, tiled=True)  12.8 us
    convert_element_type x1, local copies, waits for them, and re-layouts, local(): halfway = jnp.einsum('pab,bd->pda', df_blocks, fno_rotation, preferred_el...  11 us
    dot_general x1, matrix products, local(): jnp.einsum('pab,bd->pda', df_blocks, fno_rotation, preferred_element_type...  9.62 us
    transpose x1, local copies, waits for them, and re-layouts, local(): jnp.einsum('ptc,ptd->ctd', left_rows, right_rows, preferred_element_type=...  7.32 us
  transfers between devices with their start and end apart: 2, of which 1 were waited for; matrix products, arithmetic and copies ran while one was open for 0% of the time, Pallas kernels for 0%

commit v1 on v0

v1 whole, which is shorter than its diff:
```python
import functools

import jax
import jax.numpy as jnp
import numpy as np
from jax import lax
from jax.experimental import pallas as pl
from jax.experimental.pallas import tpu as pltpu
from jax.sharding import PartitionSpec as P

MESH = pl.DeviceIdType.MESH
BF = jnp.bfloat16
F32 = jnp.float32

ROUNDS = 4
SUB = 2
GROUPS = 4


def dot(a, b):
    return jnp.dot(a, b, preferred_element_type=F32)


def dot_nt(a, b):
    return lax.dot_general(a, b, (((1,), (1,)), ((), ())), preferred_element_type=F32)


def kernel(
    df_ref, rot_ref, pairs_ref, spread_ref, mask_ref, out_ref,
    df_v, rot_v, half_v, quad_v, pair_v, hot_v, w_v, tsend_v, town_v, trecv_v,
    zsend_v, zown_v, zrecv_v, fno_v, gsend_v, gath_v, pick_v, acc_v,
    df_sem, rot_sem, p_ssem, p_rsem, h_ssem, h_rsem, t_ssem, t_rsem,
    z_ssem, z_rsem, g_ssem, g_rsem, y_ssem, y_rsem,
):
    natural = rot_v.shape[1]
    aux = lax.axis_index("aux")
    virt = lax.axis_index("virt")
    zl, y = aux // 4, aux % 4
    x, zh, c = virt // 8, (virt // 2) % 4, virt % 2
    hrows = half_v.shape[1] // 8
    rrows = half_v.shape[1]

    def dev(zl_, y_, x_, zh_, c_):
        return (zl_ * 4 + y_, (x_ * 4 + zh_) * 2 + c_)

    def remote(src, dst, ssem, rsem, device):
        return pltpu.make_async_remote_copy(
            src_ref=src, dst_ref=dst, send_sem=ssem, recv_sem=rsem, device_id=device, device_id_type=MESH
        )

    def df_copy(i):
        return pltpu.make_async_copy(df_ref.at[pl.ds(i * rrows, rrows)], df_v.at[i], df_sem.at[i])

    rot_copy = pltpu.make_async_copy(rot_ref, rot_v, rot_sem)
    rot_copy.start()
    for i in range(ROUNDS):
        df_copy(i).start()

    xr, xl = (x + 1) % 4, (x + 3) % 4
    peers = [dev(zl, y, x, zh, 1 - c)]
    peers += [dev(zl, y, xx, zh, cc) for xx in (xr, xl) for cc in range(2)]
    peers += [dev(zl, y, x, (zh + d) % 4, c) for d in range(1, 4)]
    peers += [dev(1 - zl, y, xx, zh, cc) for xx in (x, xr, xl) for cc in range(2)]
    peers += [dev(zl, (y + d) % 4, x, zh, c) for d in range(1, 4)]
    barrier = pltpu.get_barrier_semaphore()
    for peer in peers:
        pl.semaphore_signal(barrier, inc=1, device_id=peer, device_id_type=MESH)

    row = lax.broadcasted_iota(jnp.int32, (8, 128), 0)
    tile = row % 2
    side = row // 4
    mine = jnp.where(
        side == 0,
        jnp.where(tile == 0, pairs_ref[0, 0], pairs_ref[1, 0]),
        jnp.where(tile == 0, pairs_ref[0, 1], pairs_ref[1, 1]),
    )
    pair_v[x, c, zh] = mine

    def place(col):
        u = (x + 4 - col) % 4
        j, xh = u % 2, u // 2
        return u, j, xh, (j + xh) % 2

    def quad_dst(col, q):
        u, j, xh, pq = place(col)
        jd = (q // 2 + xh) % 2
        return (xh * 2 + jd + col) % 4, q % 2

    def h_copy(i, col, d):
        u, j, xh, pq = place(col)
        q = (pq * 2 + c + d) % 4
        xd, cd = quad_dst(col, q)
        src = half_v.at[i, pl.ds(pl.multiple_of(col * 4 * hrows + q * hrows, 16), hrows)]
        dst = quad_v.at[i, col, pl.ds(pl.multiple_of((j * 2 + c) * hrows, 16), hrows)]
        if d == 0:
            return pltpu.make_async_copy(src, dst, h_rsem.at[i, col, 0])
        return remote(src, dst, h_ssem.at[i, col, d], h_rsem.at[i, col, d], dev(zl, y, xd, zh, cd))

    def half_step(i):
        df_copy(i).wait()
        half_v[i] = dot(df_v[i], rot_v[...]).astype(BF)

    def half_send(i):
        for d in (2, 3, 1, 0):
            for col in range(2):
                h_copy(i, col, d).start()

    def p_first(d):
        ref = pair_v.at[x, c, zh]
        return remote(ref, ref, p_ssem.at[d], p_rsem.at[d], dev(zl, y, x, (zh + d) % 4, c))

    def p_second(n):
        ref = pair_v.at[x, c]
        xx = (x, xr, xr, xl, xl)[n]
        cc = (1 - c, c, 1 - c, c, 1 - c)[n]
        return remote(ref, ref, p_ssem.at[4 + n], p_rsem.at[4 + n], dev(zl, y, xx, zh, cc))

    def p_third():
        ref = pair_v.at[xr]
        return remote(ref, ref, p_ssem.at[9], p_rsem.at[9], dev(zl, y, xl, zh, c))

    rot_copy.wait()
    half_step(0)
    pl.semaphore_wait(barrier, len(peers))
    half_send(0)
    for d in range(1, 4):
        p_first(d).start()
    half_step(1)
    half_send(1)
    for d in range(1, 4):
        p_first(d).wait_recv()
    for n in range(5):
        p_second(n).start()
    for n in range(5):
        p_second(n).wait_recv()
    p_third().start()

    lane = lax.broadcasted_iota(jnp.int32, (natural, 128), 1)
    col_at = lax.broadcasted_iota(jnp.int32, (natural, 128), 0)
    del lane, col_at
    pick_row = lax.broadcasted_iota(jnp.int32, (128, natural), 0)
    pick_col = lax.broadcasted_iota(jnp.int32, (128, natural), 1)
    pick_v[...] = jnp.where((pick_col == pick_row + aux * 80) & (pick_row < 80), 1.0, 0.0).astype(BF)
    acc_v[...] = jnp.zeros_like(acc_v)

    p_third().wait_recv()
    for col in range(2):
        u, j, xh, pq = place(col)
        wanted = jnp.concatenate(
            [pair_v[(2 * h + jj + col) % 4, cc, z] for h in range(2) for z in range(4) for jj in range(2) for cc in range(2)],
            axis=0,
        )
        at = lax.broadcasted_iota(jnp.int32, wanted.shape, 1)
        for n in range(natural // 128):
            hot_v[:, n * 128 : (n + 1) * 128] = jnp.where(wanted == at + n * 128, 1.0, 0.0).astype(BF)
        total = None
        for jj in range(2):
            xs = (xh * 2 + jj + col) % 4
            rows = rot_v[pl.ds(pl.multiple_of((xs * 4 + zh) * 80, 16), 80)]
            sel = dot_nt(hot_v[...], rows).astype(BF)
            part = dot(sel, spread_ref[jj])
            total = part if total is None else total + part
        w_v[col] = (total * mask_ref[...]).astype(BF)

    def t_copy(i, col):
        u, j, xh, pq = place(col)
        xd = jnp.where(j == 1, xr, xl)
        return remote(tsend_v.at[i, col], trecv_v.at[i, col], t_ssem.at[i, col], t_rsem.at[i, col], dev(zl, y, xd, zh, c))

    def t_step(i, col):
        u, j, xh, pq = place(col)
        for d in range(4):
            if d == 0:
                h_copy(i, col, 0).wait()
            else:
                h_copy(i, col, d).wait_recv()
        other = pl.ds(pl.multiple_of((1 - xh) * 128, 128), 128)
        own = pl.ds(pl.multiple_of(xh * 128, 128), 128)
        tsend_v[i, col] = dot(w_v[col, other], quad_v[i, col]).astype(BF)
        t_copy(i, col).start()
        town_v[i, col] = dot(w_v[col, own], quad_v[i, col])

    def z_copy(i, col, d):
        return remote(
            zsend_v.at[i, col, d - 1], zrecv_v.at[i, col, d - 1],
            z_ssem.at[i, col, d - 1], z_rsem.at[i, col, d - 1], dev(zl, y, x, (zh + d) % 4, c),
        )

    def z_step(i, col):
        t_copy(i, col).wait_recv()
        for d in (2, 1, 3, 0):
            rows = pl.ds(pl.multiple_of((zh + d) % 4 * 32, 32), 32)
            value = town_v[i, col, rows] + trecv_v[i, col, rows].astype(F32)
            if d:
                zsend_v[i, col, d - 1] = value.astype(BF)
                z_copy(i, col, d).start()
            else:
                zown_v[i, col] = value

    def g_copy(col, m, d):
        u, j, xh, pq = place(col)
        slot = (zl * 2 + j) * 2 + c
        to = (slot + d) % 8
        zd, jd, cd = to // 4, (to // 2) % 2, to % 2
        g = col * 2 + m
        src = gsend_v.at[g, pl.ds(pl.multiple_of((jd * 2 + cd) * 16, 16), 16)]
        dst = gath_v.at[g, y, pl.ds(pl.multiple_of(slot * 16, 16), 16)]
        if d == 0:
            return pltpu.make_async_copy(src, dst, g_rsem.at[g, 0])
        return remote(src, dst, g_ssem.at[g, d], g_rsem.at[g, d], dev(zd, y, (xh * 2 + jd + col) % 4, zh, cd))

    def f_step(i, col):
        for d in range(1, 4):
            z_copy(i, col, d).wait_recv()
        value = zown_v[i, col] + (zrecv_v[i, col, 0].astype(F32) + zrecv_v[i, col, 1].astype(F32)) + zrecv_v[
            i, col, 2
        ].astype(F32)
        fno_v[col * 2 + i // 2, :, i % 2] = value.reshape(4, 8, natural)

    def g_step(m, col):
        g = col * 2 + m
        gsend_v[g] = fno_v[g].reshape(64, natural).astype(BF)
        for d in range(8):
            g_copy(col, m, d).start()

    def y_copy(g, d):
        ref = gath_v.at[g, y]
        return remote(ref, ref, y_ssem.at[g, d - 1], y_rsem.at[g, d - 1], dev(zl, (y + d) % 4, x, zh, c))

    def y_step(m, col):
        g = col * 2 + m
        g_copy(col, m, 0).wait()
        for d in range(1, 8):
            g_copy(col, m, d).wait_recv()
        for d in (2, 1, 3):
            y_copy(g, d).start()

    def out_step(m, col):
        g = col * 2 + m
        for d in range(1, 4):
            y_copy(g, d).wait_recv()
        rows = gath_v[g].reshape(512, natural)
        left = pltpu.roll(dot_nt(pick_v[...], rows), 4, 1)
        at = lax.broadcasted_iota(jnp.int32, left.shape, 1)
        for t in range(2):
            here = (at % 8 >= 4) & (at % 2 == t)
            acc_v[t] += dot(jnp.where(here, left, 0.0).astype(BF), rows)

    def body(it, carry):
        @pl.when(it < ROUNDS)
        def _():
            for col in range(2):
                t_step(it, col)

        @pl.when(it + 2 < ROUNDS)
        def _():
            half_step(it + 2)
            half_send(it + 2)

        @pl.when((it >= 1) & (it < ROUNDS + 1))
        def _():
            for col in range(2):
                z_step(it - 1, col)

        @pl.when((it >= 2) & (it < ROUNDS + 2))
        def _():
            for col in range(2):
                f_step(it - 2, col)

        @pl.when((it == 3) | (it == 5))
        def _():
            for col in range(2):
                g_step((it - 3) // 2, col)

        @pl.when((it == 4) | (it == 6))
        def _():
            for col in range(2):
                y_step((it - 4) // 2, col)

        @pl.when((it == 5) | (it == 7))
        def _():
            for col in range(2):
                out_step((it - 5) // 2, col)

        return carry

    lax.fori_loop(0, 8, body, 0)
    out_ref[...] = acc_v[:, :80]

    for d in range(1, 4):
        p_first(d).wait_send()
    for n in range(5):
        p_second(n).wait_send()
    p_third().wait_send()

    def drain(i, carry):
        for col in range(2):
            for d in range(1, 4):
                h_copy(i, col, d).wait_send()
                z_copy(i, col, d).wait_send()
            t_copy(i, col).wait_send()
        return carry

    lax.fori_loop(0, ROUNDS, drain, 0)

    def drain_groups(m, carry):
        for col in range(2):
            for d in range(1, 8):
                g_copy(col, m, d).wait_send()
            for d in range(1, 4):
                y_copy(col * 2 + m, d).wait_send()
        return carry

    lax.fori_loop(0, 2, drain_groups, 0)


def constants():
    k = np.arange(4 * SUB * 40)
    dev, fun, orb = k // (SUB * 40), (k // 40) % SUB, k % 40
    a = np.arange(80)
    spread = np.stack(
        [(dev[None] == 2 * jj + a[:, None] // 40) & (orb[None] == a[:, None] % 40) for jj in range(2)]
    )
    r = np.arange(256)
    mask = ((r[:, None] // 2) % SUB) == fun[None]
    return spread.astype(np.float32), mask.astype(np.float32)


def solution(mesh):
    spread, mask = constants()

    def local(df_blocks, fno_rotation, tile_pairs):
        aux_n, orbs, nv = df_blocks.shape
        nf = fno_rotation.shape[1]
        rows = aux_n * orbs // ROUNDS
        vm = pltpu.VMEM
        dma = pltpu.SemaphoreType.DMA
        out = pl.pallas_call(
            kernel,
            name="tiles",
            out_shape=jax.ShapeDtypeStruct((2, 80, nf), F32),
            in_specs=[
                pl.BlockSpec(memory_space=pl.ANY),
                pl.BlockSpec(memory_space=pl.ANY),
                pl.BlockSpec(memory_space=pltpu.SMEM),
                pl.BlockSpec(memory_space=pltpu.VMEM),
                pl.BlockSpec(memory_space=pltpu.VMEM),
            ],
            out_specs=pl.BlockSpec(memory_space=pltpu.VMEM),
            scratch_shapes=[
                vm((ROUNDS, rows, nv), BF),
                vm((nv, nf), BF),
                vm((ROUNDS, rows, nf), BF),
                vm((ROUNDS, 2, rows // 2, nf), BF),
                vm((4, 2, 4, 8, 128), jnp.int32),
                vm((256, nf), BF),
                vm((2, 256, 4 * SUB * 40), BF),
                vm((ROUNDS, 2, 128, nf), BF),
                vm((ROUNDS, 2, 128, nf), F32),
                vm((ROUNDS, 2, 128, nf), BF),
                vm((ROUNDS, 2, 3, 32, nf), BF),
                vm((ROUNDS, 2, 32, nf), F32),
                vm((ROUNDS, 2, 3, 32, nf), BF),
                vm((GROUPS, 4, 2, 8, nf), F32),
                vm((GROUPS, 64, nf), BF),
                vm((GROUPS, 4, 128, nf), BF),
                vm((128, nf), BF),
                vm((2, 128, nf), F32),
                dma((ROUNDS,)),
                dma(()),
                dma((10,)), dma((10,)),
                dma((ROUNDS, 2, 4)), dma((ROUNDS, 2, 4)),
                dma((ROUNDS, 2)), dma((ROUNDS, 2)),
                dma((ROUNDS, 2, 3)), dma((ROUNDS, 2, 3)),
                dma((GROUPS, 8)), dma((GROUPS, 8)),
                dma((GROUPS, 3)), dma((GROUPS, 3)),
            ],
            compiler_params=pltpu.CompilerParams(
                collective_id=0, has_side_effects=True, vmem_limit_bytes=58 * 2**20
            ),
        )(
            df_blocks.reshape(aux_n * orbs, nv),
            fno_rotation,
            tile_pairs,
            jnp.asarray(spread, BF),
            jnp.asarray(mask, F32),
        )
        return jnp.transpose(out, (1, 0, 2))

    placed = (P("aux", "virt", None), P(), P("virt", None))
    return jax.shard_map(local, mesh=mesh, in_specs=placed, out_specs=P("aux", "virt", None), check_vma=False)
```

time: 313 us -> 99.5 us (0.32)
  the two profiles are of different devices: /device:TPU:1 before, /device:TPU:66 now
where the time goes in v1:
time: 99.5 us; the launch traced here: 99.4 us
  Pallas kernels  97.4 us (98%)
  local copies, waits for them, and re-layouts  1.96 us (2%)
    pallas_call x1, Pallas kernels, local(): pl.pallas_call(kernel, name='tiles', out_shape=jax.ShapeDtypeStruct((2, 8...  97.4 us

profile of v1, /device:TPU:66, one launch (start us, length us, event | category | flops | bytes accessed | tf_op | source)
XLA Modules:
  0.0 99.4 jit_solution(8462500050220985668)
XLA Ops:
  0.0 97.4 %tiles.1 = f32[2,80,640]{2,1,0:T(8,128)} custom-call(bf16[2560,1280]{1,0:T(8,128)(2,1)} %bitcast.2, bf16[1280,640]{1,0:T(8,128)(2,1)} %rot_ref.1, s32[2,2]{1,0:T(2,128)} %pairs_ref.1, bf16[2,80,320]{2,1,0:T(8,128)(2,1)} %constant.4.clone.spread_ref, f32[256,320]{1,0:T(8,128)} %constant.5.clone.mask_ref), custom_call_target="tpu_custom_call" | custom-call | tf_op jit(solution)/shard_map/tiles/pallas_call | solution.py:338
  97.4 2.0 %copy.6 = f32[80,2,640]{2,1,0:T(2,128)} copy(f32[80,2,640]{2,0,1:T(8,128)} %bitcast.3) | data formatting | bytes 819200 | tf_op jit(solution)/shard_map/transpose | solution.py:388

commit v2 on v0

v2 whole, which is shorter than its diff:
```python
import jax
import jax.numpy as jnp
import numpy as np
from jax import lax
from jax.experimental import pallas as pl
from jax.experimental.pallas import tpu as pltpu
from jax.sharding import PartitionSpec as P

MESH = pl.DeviceIdType.MESH
BF = jnp.bfloat16
F32 = jnp.float32

ROUNDS = 4
Z_FIRST = ()
FIRST, SECOND = (2, 1, 0), (3,)
LATE = ()
SPLIT = (3,)
PLAN = (
    "t0", "h2", "t1", "h3", "a0", "b0", "t2", "a1", "f0", "b1", "t3", "a2", "f1", "y0", "a3", "b2", "b3",
    "y1", "f2", "f3", "o0", "y2", "y3", "o1", "o2", "d0", "o3",
)
SUB = 2


def pieces(i):
    return ((0, 384), (384, 256)) if i in SPLIT else ((0, 640),)


def dot(a, b):
    return jnp.dot(a, b, preferred_element_type=F32)


def dot_nt(a, b):
    return lax.dot_general(a, b, (((1,), (1,)), ((), ())), preferred_element_type=F32)


def kernel(
    df_ref, rot_ref, pairs_ref, spread_ref, mask_ref, out_ref,
    spread_v, mask_v, df_v, rot_v, half_v, quad_v, pair_v, pack_v, hot_v, w_v, tsend_v, town_v, trecv_v,
    asend_v, aown_v, arecv_v, bsend_v, bown_v, brecv_v, gsend_v, gath_v, order_v, pick_v, rows_v, ysend_v, acc_v,
    c_sem, df_sem, rot_sem, p_ssem, p_rsem, h_ssem, h_rsem, t_ssem, t_rsem,
    a_ssem, a_rsem, b_ssem, b_rsem, g_ssem, g_rsem, y_ssem, y_rsem, o_sem,
):
    natural = rot_v.shape[1]
    aux = lax.axis_index("aux")
    virt = lax.axis_index("virt")
    zl, y = aux // 4, aux % 4
    x, zh, c = virt // 8, (virt // 2) % 4, virt % 2
    hrows = half_v.shape[1] // 8
    rrows = half_v.shape[1]

    def dev(zl_, y_, x_, zh_, c_):
        return (zl_ * 4 + y_, (x_ * 4 + zh_) * 2 + c_)

    def remote(src, dst, ssem, rsem, device):
        return pltpu.make_async_remote_copy(
            src_ref=src, dst_ref=dst, send_sem=ssem, recv_sem=rsem, device_id=device, device_id_type=MESH
        )

    def landed(ref, sem):
        pltpu.make_async_copy(ref, ref, sem).wait()

    def df_copy(i):
        return pltpu.make_async_copy(df_ref.at[pl.ds(i * rrows, rrows)], df_v.at[i], df_sem.at[i])

    rot_copy = pltpu.make_async_copy(rot_ref, rot_v, rot_sem)
    rot_copy.start()
    df_copy(0).start()

    xr, xl = (x + 1) % 4, (x + 3) % 4
    xo = (x + 2) % 4
    peers = [dev(zl, y, x, zh, 1 - c)]
    peers += [dev(zl, y, xx, zh, cc) for xx in (xr, xl, xo) for cc in range(2)]
    peers += [dev(zl, y, x, (zh + d) % 4, c) for d in range(1, 4)]
    peers += [dev(1 - zl, y, xx, zh, cc) for xx in (x, xr, xl) for cc in range(2)]
    peers += [dev(zl, (y + d) % 4, x, zh, c) for d in range(1, 4)]
    barrier = pltpu.get_barrier_semaphore()
    for peer in peers:
        pl.semaphore_signal(barrier, inc=1, device_id=peer, device_id_type=MESH)

    row = lax.broadcasted_iota(jnp.int32, (8, 128), 0)
    tile = row % 2
    side = row // 4
    mine = jnp.where(
        side == 0,
        jnp.where(tile == 0, pairs_ref[0, 0], pairs_ref[1, 0]),
        jnp.where(tile == 0, pairs_ref[0, 1], pairs_ref[1, 1]),
    )
    pair_v[zh, x * 2 + c] = mine

    def place(col):
        u = (x + 4 - col) % 4
        j, xh = u % 2, u // 2
        return u, j, xh, (j + xh) % 2

    def quad_dst(col, q):
        u, j, xh, pq = place(col)
        jd = (q // 2 + xh) % 2
        return (xh * 2 + jd + col) % 4, q % 2

    def h_copy(i, col, d):
        u, j, xh, pq = place(col)
        q = (pq + d // 2) % 2 * 2 + (c + d % 2) % 2
        xd, cd = quad_dst(col, q)
        src = half_v.at[i, pl.ds(pl.multiple_of(col * 4 * hrows + q * hrows, 16), hrows)]
        dst = quad_v.at[i, col, pl.ds(pl.multiple_of((j * 2 + c) * hrows, 16), hrows)]
        if d == 0:
            return pltpu.make_async_copy(src, dst, h_rsem.at[i, col])
        return remote(src, dst, h_ssem, h_rsem.at[i, col], dev(zl, y, xd, zh, cd))

    def half_step(i):
        df_copy(i).wait()
        half_v[i] = dot(df_v[i], rot_v[...]).astype(BF)

    def half_send(i, ds=(2, 3, 1, 0)):
        for d in ds:
            for col in range(2):
                h_copy(i, col, d).start()

    def p_first(n):
        ref = pair_v.at[zh, x * 2 + c]
        xx = (x, xr, xr, xl, xl, xo, xo)[n]
        cc = (1 - c, c, 1 - c, c, 1 - c, c, 1 - c)[n]
        return remote(ref, ref, p_ssem.at[0], p_rsem.at[0], dev(zl, y, xx, zh, cc))

    def p_second(d):
        ref = pack_v.at[zh]
        return remote(ref, ref, p_ssem.at[1], p_rsem.at[1], dev(zl, y, x, (zh + d) % 4, c))

    def p_step():
        landed(pair_v.at[0, pl.ds(0, 7)], p_rsem.at[0])
        lane = lax.broadcasted_iota(jnp.int32, (8, 128), 1)
        packed = pair_v[zh, 0]
        for k in range(1, 8):
            packed = jnp.where(lane >= 16 * k, pair_v[zh, k], packed)
        pack_v[zh] = packed
        for d in (2, 1, 3):
            p_second(d).start()

    pl.semaphore_wait(barrier, len(peers))
    for n in range(7):
        p_first(n).start()
    rot_copy.wait()
    const_copies = (
        pltpu.make_async_copy(spread_ref, spread_v, c_sem.at[0]),
        pltpu.make_async_copy(mask_ref, mask_v, c_sem.at[1]),
    )
    for copy in const_copies:
        copy.start()
    for i in range(1, ROUNDS):
        df_copy(i).start()
    half_step(0)
    half_send(0)
    p_step()
    half_step(1)
    half_send(1, FIRST if 1 in LATE else FIRST + SECOND)

    def p_last_step():
        landed(pack_v.at[pl.ds(0, 3)], p_rsem.at[1])

    p_last_step()

    def w_step():
        blocks = [
            [jnp.broadcast_to(pack_v[z][:, 16 * k : 16 * k + 1], (8, 128)) for k in range(8)] for z in range(4)
        ]
        for col in range(2):
            u, j, xh, pq = place(col)
            wanted = jnp.concatenate(
                [blocks[(z + 1 + col) % 4][(2 * h + jj + col) % 4 * 2 + cc] for h in range(2) for z in range(4) for jj in range(2) for cc in range(2)],
                axis=0,
            )
            at = lax.broadcasted_iota(jnp.int32, wanted.shape, 1)
            for n in range(natural // 128):
                hot_v[:, n * 128 : (n + 1) * 128] = jnp.where(wanted == at + n * 128, 1.0, 0.0).astype(BF)
            total = None
            for jj in range(2):
                xs = (xh * 2 + jj + col) % 4
                rows = rot_v[pl.ds(pl.multiple_of((xs * 4 + zh) * 80, 16), 80)]
                sel = dot_nt(hot_v[...], rows).astype(BF)
                part = dot(sel, spread_v[jj])
                total = part if total is None else total + part
            w_v[col] = (total * mask_v[...].astype(F32)).astype(BF)

    for copy in const_copies:
        copy.wait()
    w_step()

    def zplace(col):
        uz = (zh + 4 - col) % 4
        return uz, (uz + 3) % 4

    def x_partner(col):
        return dev(zl, y, jnp.where(place(col)[1] == 1, xr, xl), zh, c)

    def z_partner(col):
        uz, p = zplace(col)
        return dev(zl, y, x, (uz + 1 - 2 * (uz % 2) + col) % 4, c)

    def t_copy(i, col, n):
        to = z_partner(col) if i in Z_FIRST else x_partner(col)
        at = pl.ds(*pieces(i)[n])
        return remote(tsend_v.at[i, col, :, at], trecv_v.at[i, col, :, at], t_ssem, t_rsem.at[i, col, n], to)

    def w_rows(i, col, own):
        xh, s = place(col)[2], zplace(col)[1] // 2
        if i not in Z_FIRST:
            return w_v[col, pl.ds(pl.multiple_of((xh if own else 1 - xh) * 128, 128), 128)]
        s = s if own else 1 - s
        return jnp.concatenate([w_v[col, pl.ds(pl.multiple_of((2 * h + s) * 64, 64), 64)] for h in range(2)], axis=0)

    def t_step(i, col, n):
        if n == 0:
            landed(quad_v.at[i, col], h_rsem.at[i, col])
        at = pl.ds(*pieces(i)[n])
        tsend_v[i, col, :, at] = dot(w_rows(i, col, False), quad_v[i, col, :, at]).astype(BF)
        t_copy(i, col, n).start()
        town_v[i, col, :, at] = dot(w_rows(i, col, True), quad_v[i, col, :, at])

    def a_copy(i, col, n):
        to = x_partner(col) if i in Z_FIRST else z_partner(col)
        at = pl.ds(*pieces(i)[n])
        return remote(asend_v.at[i, col, :, at], arecv_v.at[i, col, :, at], a_ssem, a_rsem.at[i, col, n], to)

    def a_step(i, col, n):
        t_copy(i, col, n).wait_recv()
        half = place(col)[2] if i in Z_FIRST else zplace(col)[1] // 2
        at = pl.ds(*pieces(i)[n])
        other = pl.ds(pl.multiple_of((1 - half) * 64, 64), 64)
        own = pl.ds(pl.multiple_of(half * 64, 64), 64)
        asend_v[i, col, :, at] = (town_v[i, col, other, at] + trecv_v[i, col, other, at].astype(F32)).astype(BF)
        a_copy(i, col, n).start()
        aown_v[i, col, :, at] = town_v[i, col, own, at] + trecv_v[i, col, own, at].astype(F32)

    def b_copy(i, col, n):
        uz, p = zplace(col)
        zd = (p + 2 - 2 * (p % 2) + col) % 4
        at = pl.ds(*pieces(i)[n])
        return remote(
            bsend_v.at[i, col, :, at], brecv_v.at[i, col, :, at], b_ssem, b_rsem.at[i, col, n], dev(zl, y, x, zd, c)
        )

    def b_step(i, col, n):
        a_copy(i, col, n).wait_recv()
        uz, p = zplace(col)
        at = pl.ds(*pieces(i)[n])
        other = pl.ds(pl.multiple_of((1 - p % 2) * 32, 32), 32)
        own = pl.ds(pl.multiple_of(p % 2 * 32, 32), 32)
        bsend_v[i, col, :, at] = (aown_v[i, col, other, at] + arecv_v[i, col, other, at].astype(F32)).astype(BF)
        b_copy(i, col, n).start()
        bown_v[i, col, :, at] = aown_v[i, col, own, at] + arecv_v[i, col, own, at].astype(F32)

    def g_copy(i, col, d):
        u, j, xh, pq = place(col)
        slot = (zl * 2 + j) * 2 + c
        to = (slot + d) % 8
        zd, jd, cd = to // 4, (to // 2) % 2, to % 2
        src = gsend_v.at[i, col, zd, pl.ds(pl.multiple_of((jd * 2 + cd) * 16, 16), 16)]
        dst = gath_v.at[i * 2 + col, pl.ds(pl.multiple_of(slot * 16, 16), 16)]
        if d == 0:
            return pltpu.make_async_copy(src, dst, g_rsem.at[i, col])
        return remote(src, dst, g_ssem, g_rsem.at[i, col], dev(zd, y, (xh * 2 + jd + col) % 4, zh, cd))

    def f_step(i, col):
        for n in range(len(pieces(i))):
            b_copy(i, col, n).wait_recv()
        value = bown_v[i, col] + brecv_v[i, col].astype(F32)
        tiles = [value[:, 128 * n : 128 * (n + 1)] for n in range(5)]
        lower = lax.broadcasted_iota(jnp.int32, (32, 128), 0) % 8 >= 4
        for w in range(2):
            win, rest = tiles[2 * w : 2 * w + 3], (tiles[3:] if w == 0 else tiles[:2])
            shared = jnp.where(lower, rest[0], pltpu.roll(rest[1], 28, 0))
            upper = jnp.concatenate([win[0], win[1]], axis=1).reshape(4, 8, 256)
            under = jnp.concatenate([win[2], shared], axis=1).reshape(4, 8, 256)
            gsend_v[i, col, w] = jnp.concatenate([upper, under], axis=1).reshape(64, 256).astype(BF)
        for d in (4, 5, 6, 7, 2, 3, 1, 0):
            g_copy(i, col, d).start()

    def y_copy(i, col, d):
        return remote(
            ysend_v.at[i, col, d - 1], rows_v.at[y, i, col],
            y_ssem, y_rsem.at[i], dev(zl, (y + d) % 4, x, zh, c),
        )

    def y_step(i, col):
        landed(gath_v.at[i * 2 + col], g_rsem.at[i, col])
        packed = gath_v[i * 2 + col]
        upper = dot(order_v[0], packed).astype(BF)
        under = dot(order_v[1], packed).astype(BF)
        win = [upper[:32, :128], upper[:32, 128:], under[:32, :128]]
        rest = [under[:32, 128:], under[32:, 128:]]
        right = jnp.where(zl == 0, jnp.concatenate(win + rest, axis=1), jnp.concatenate(rest + win, axis=1))
        pick_copy = dot(jnp.concatenate([upper[32:], under[32:, :128]], axis=1), pick_v[...]).astype(BF)
        lefts = [pick_copy[:, 128 * n : 128 * (n + 1)] for n in range(4)]
        for d in (2, 1, 3, 0):
            to = (y + d) % 4
            left = jnp.where(to < 2, jnp.where(to == 0, lefts[0], lefts[1]), jnp.where(to == 2, lefts[2], lefts[3]))
            if d:
                ysend_v[i, col, d - 1, :, :natural] = right
                ysend_v[i, col, d - 1, :, natural:] = left
                y_copy(i, col, d).start()
            else:
                rows_v[y, i, col, :, :natural] = right
                rows_v[y, i, col, :, natural:] = left

    def out_step(i):
        landed(rows_v.at[pl.ds(0, 3), i], y_rsem.at[i])
        both = rows_v[:, i].reshape(256, natural + 128)
        left = both[:, natural:]
        parity = lax.broadcasted_iota(jnp.int32, left.shape, 0) % 2
        zero = jnp.zeros_like(left)
        left = jnp.concatenate([jnp.where(parity == t, left, zero) for t in range(2)], axis=1)
        acc_v[...] += lax.dot_general(
            left, both[:, :natural], (((0,), (0,)), ((), ())), preferred_element_type=F32
        )

    def one_hots():
        to = lax.broadcasted_iota(jnp.int32, (64, 128), 0)
        at = lax.broadcasted_iota(jnp.int32, (64, 128), 1)
        source = (to % 32) // 4 * 16 + to % 4 + jnp.where(to < 32, 4, 0)
        for n in range(2):
            order_v[n] = jnp.where(at == source + 8 * n, 1.0, 0.0).astype(BF)
        at = lax.broadcasted_iota(jnp.int32, (384, 512), 0)
        to = lax.broadcasted_iota(jnp.int32, (384, 512), 1)
        source = (zl * 4 + to // 128) * 80 + to % 128 - zl * 256
        pick_v[...] = jnp.where((at == source) & (to % 128 < 80), 1.0, 0.0).astype(BF)
        acc_v[...] = jnp.zeros_like(acc_v)

    def drain_step():
        landed(pair_v.at[0, pl.ds(0, 7)], p_ssem.at[0])
        landed(pack_v.at[pl.ds(0, 3)], p_ssem.at[1])
        landed(half_v.at[pl.ds(0, 3)], h_ssem)
        landed(tsend_v, t_ssem)
        landed(asend_v, a_ssem)
        landed(bsend_v, b_ssem)
        landed(gath_v.at[pl.ds(0, 2 * ROUNDS - 1)], g_ssem)

    steps = {"t": t_step, "a": a_step, "b": b_step, "f": f_step, "y": y_step}
    one_hots()
    for token in PLAN:
        name, i = token[0], int(token[1])
        if name == "h":
            half_step(i)
            half_send(i, FIRST if i in LATE else FIRST + SECOND)
        elif name == "s":
            half_send(i, SECOND)
        elif name == "o":
            out_step(i)
        elif name == "d":
            drain_step()
        elif name in "tab":
            for n in (int(token[2]),) if len(token) > 2 else range(len(pieces(i))):
                for col in range(2):
                    steps[name](i, col, n)
        else:
            for col in range(2):
                steps[name](i, col)

    def out_copy(t, n):
        rows = 80 // 1
        return pltpu.make_async_copy(
            acc_v.at[pl.ds(128 * t + n * rows, rows)],
            out_ref.at[pl.ds(n * rows, rows), pl.ds(natural * t, natural)],
            o_sem.at[t],
        )

    def w_out_step():
        for t in range(2):
            for n in range(1):
                out_copy(t, n).start()
        for t in range(2):
            for n in range(1):
                out_copy(t, n).wait()

    w_out_step()
    landed(ysend_v, y_ssem)


def constants():
    k = np.arange(4 * SUB * 40)
    dev, fun, orb = k // (SUB * 40), (k // 40) % SUB, k % 40
    a = np.arange(80)
    spread = np.stack(
        [(dev[None] == 2 * jj + a[:, None] // 40) & (orb[None] == a[:, None] % 40) for jj in range(2)]
    )
    r = np.arange(256)
    mask = ((r[:, None] // 2) % SUB) == fun[None]
    return spread.astype(np.float32), mask.astype(np.float32)


def solution(mesh):
    spread, mask = constants()

    def local(df_blocks, fno_rotation, tile_pairs):
        aux_n, orbs, nv = df_blocks.shape
        nf = fno_rotation.shape[1]
        rows = aux_n * orbs // ROUNDS
        vm = pltpu.VMEM
        dma = pltpu.SemaphoreType.DMA
        out = pl.pallas_call(
            kernel,
            name="tiles",
            out_shape=jax.ShapeDtypeStruct((80, 2 * nf), F32),
            in_specs=[
                pl.BlockSpec(memory_space=pl.ANY),
                pl.BlockSpec(memory_space=pl.ANY),
                pl.BlockSpec(memory_space=pltpu.SMEM),
                pl.BlockSpec(memory_space=pl.ANY),
                pl.BlockSpec(memory_space=pl.ANY),
            ],
            out_specs=pl.BlockSpec(memory_space=pl.ANY),
            scratch_shapes=[
                vm((2, 80, 4 * SUB * 40), BF),
                vm((256, 4 * SUB * 40), BF),
                vm((ROUNDS, rows, nv), BF),
                vm((nv, nf), BF),
                vm((ROUNDS, rows, nf), BF),
                vm((ROUNDS, 2, rows // 2, nf), BF),
                vm((4, 8, 8, 128), jnp.int32),
                vm((4, 8, 128), jnp.int32),
                vm((256, nf), BF),
                vm((2, 256, 4 * SUB * 40), BF),
                vm((ROUNDS, 2, 128, nf), BF),
                vm((ROUNDS, 2, 128, nf), F32),
                vm((ROUNDS, 2, 128, nf), BF),
                vm((ROUNDS, 2, 64, nf), BF),
                vm((ROUNDS, 2, 64, nf), F32),
                vm((ROUNDS, 2, 64, nf), BF),
                vm((ROUNDS, 2, 32, nf), BF),
                vm((ROUNDS, 2, 32, nf), F32),
                vm((ROUNDS, 2, 32, nf), BF),
                vm((ROUNDS, 2, 2, 64, 256), BF),
                vm((ROUNDS * 2, 128, 256), BF),
                vm((2, 64, 128), BF),
                vm((384, 512), BF),
                vm((4, ROUNDS, 2, 32, nf + 128), BF),
                vm((ROUNDS, 2, 3, 32, nf + 128), BF),
                vm((256, nf), F32),
                dma((2,)),
                dma((ROUNDS,)),
                dma(()),
                dma((2,)), dma((2,)),
                dma(()), dma((ROUNDS, 2)),
                dma(()), dma((ROUNDS, 2, 2)),
                dma(()), dma((ROUNDS, 2, 2)),
                dma(()), dma((ROUNDS, 2, 2)),
                dma(()), dma((ROUNDS, 2)),
                dma(()), dma((ROUNDS,)),
                dma((2,)),
            ],
            compiler_params=pltpu.CompilerParams(
                collective_id=0, has_side_effects=True, vmem_limit_bytes=59392 * 2**10
            ),
        )(
            df_blocks.reshape(aux_n * orbs, nv),
            fno_rotation,
            tile_pairs,
            jnp.asarray(spread, BF),
            jnp.asarray(mask, BF),
        )
        return out.reshape(80, 2, nf)

    placed = (P("aux", "virt", None), P(), P("virt", None))
    return jax.shard_map(local, mesh=mesh, in_specs=placed, out_specs=P("aux", "virt", None), check_vma=False)
```

time: 313 us -> 74.8 us (0.24)
  blocking collectives: 127 us -> 0 us
  waiting for transfers between devices: 89.2 us -> 0 us
  Pallas kernels: 0 us -> 72.7 us
  local copies, waits for them, and re-layouts: 50.2 us -> 1.97 us
  matrix products: 18.3 us -> 0 us
  between operations: 14.1 us -> 0.01 us
  starting transfers between devices: 12.8 us -> 0 us
    all_gather x1 -> x0, blocking collectives: 110 us -> none  [local(): pairs_all = lax.all_gather(tile_pairs, 'virt', axis=0, tiled=True)]
    unnamed x2 -> x0, waiting for transfers between devices: 89.2 us -> none
    pallas_call x0 -> x1, Pallas kernels: none -> 72.7 us  [local(): pl.pallas_call(kernel, name='tiles', out_shape=jax.ShapeDtypeStruct((80,...]
    unnamed x12 -> x0, local copies, waits for them, and re-layouts: 22.8 us -> none
    dot_general x3 -> x0, matrix products: 18.3 us -> none  [the longest x1 9.62 us: local(): jnp.einsum('pab,bd->pda', df_blocks, fno_rotation, preferred_element_type...]
    all_to_all x1 -> x0, blocking collectives: 17.7 us -> none  [local(): lax.all_to_all(picked, 'virt', split_axis=1, concat_axis=2, tiled=True)]
    all_to_all x1 -> x0, starting transfers between devices: 12.8 us -> none  [local(): lax.all_to_all(halfway, 'virt', split_axis=1, concat_axis=2, tiled=True)]
    convert_element_type x2 -> x0, local copies, waits for them, and re-layouts: 11.5 us -> none  [the longest x1 11 us: local(): halfway = jnp.einsum('pab,bd->pda', df_blocks, fno_rotation, preferred_el...]
  transfers between devices with their start and end apart: 2 -> 0, of which waited for: 1 -> 0; matrix products, arithmetic and copies ran while one was open for 0% -> 0% of each run, Pallas kernels for 0% -> 0%
where the time goes in v2:
time: 74.8 us; the launch traced here: 74.7 us
  Pallas kernels  72.7 us (97%)
  local copies, waits for them, and re-layouts  1.97 us (3%)
    pallas_call x1, Pallas kernels, local(): pl.pallas_call(kernel, name='tiles', out_shape=jax.ShapeDtypeStruct((80,...  72.7 us
    reshape x1, local copies, waits for them, and re-layouts, local(): return out.reshape(80, 2, nf)  1.97 us

profile of v2, /device:TPU:1, one launch (start us, length us, event | category | flops | bytes accessed | tf_op | source)
XLA Modules:
  0.0 74.7 jit_solution(11647440360943677839)
XLA Ops:
  0.0 72.7 %tiles.1 = f32[80,1280]{1,0:T(8,128)} custom-call(bf16[2560,1280]{1,0:T(8,128)(2,1)} %bitcast.1, bf16[1280,640]{1,0:T(8,128)(2,1)} %rot_ref.1, s32[2,2]{1,0:T(2,128)} %pairs_ref.1, bf16[2,80,320]{2,1,0:T(8,128)(2,1)} %constant.4.clone.spread_ref, bf16[256,320]{1,0:T(8,128)(2,1)} %constant.5.clone.mask_ref), custom_call_target="tpu_custom_call" | custom-call | tf_op jit(solution)/shard_map/tiles/pallas_call | solution.py:400
  72.7 2.0 %reshape.7 = f32[80,2,640]{2,1,0:T(2,128)} reshape(f32[80,1280]{1,0:T(8,128)} %tiles.1) | data formatting | bytes 819200 | tf_op jit(solution)/shard_map/reshape | solution.py:461

commit v3 on v2

--- a/solution.py
+++ b/solution.py
@@ -11,13 +11,13 @@
 F32 = jnp.float32
 
 ROUNDS = 4
-Z_FIRST = ()
+Z_ROUNDS = (1,)
 FIRST, SECOND = (2, 1, 0), (3,)
-LATE = ()
-SPLIT = (3,)
+LATE = (2,)
+SPLIT = (0, 1, 2, 3)
 PLAN = (
-    "t0", "h2", "t1", "h3", "a0", "b0", "t2", "a1", "f0", "b1", "t3", "a2", "f1", "y0", "a3", "b2", "b3",
-    "y1", "f2", "f3", "o0", "y2", "y3", "o1", "o2", "d0", "o3",
+    "h0", "h3", "p0", "h1", "w0", "t0", "h2", "t3", "a0", "s2", "b0", "a3", "w1", "t2", "c0", "f0", "t1",
+    "b3", "a2", "f3", "y0", "a1", "b2", "b1", "y3", "f2", "f1", "o0", "y2", "o3", "y1", "o2", "d0", "o1",
 )
 SUB = 2
 
@@ -72,6 +72,8 @@
     peers = [dev(zl, y, x, zh, 1 - c)]
     peers += [dev(zl, y, xx, zh, cc) for xx in (xr, xl, xo) for cc in range(2)]
     peers += [dev(zl, y, x, (zh + d) % 4, c) for d in range(1, 4)]
+    peers += [dev(zl, y, x, (zh + d) % 4, 1 - c) for d in (1, 3)]
+    peers += [dev(1 - zl, y, x, (zh + d) % 4, cc) for d in (1, 3) for cc in range(2)]
     peers += [dev(1 - zl, y, xx, zh, cc) for xx in (x, xr, xl) for cc in range(2)]
     peers += [dev(zl, (y + d) % 4, x, zh, c) for d in range(1, 4)]
     barrier = pltpu.get_barrier_semaphore()
@@ -88,25 +90,33 @@
     )
     pair_v[zh, x * 2 + c] = mine
 
-    def place(col):
-        u = (x + 4 - col) % 4
-        j, xh = u % 2, u // 2
-        return u, j, xh, (j + xh) % 2
-
-    def quad_dst(col, q):
-        u, j, xh, pq = place(col)
-        jd = (q // 2 + xh) % 2
-        return (xh * 2 + jd + col) % 4, q % 2
+    def to_ring(i, first, second, core, zl_=zl):
+        return dev(zl_, y, second, first, core) if i in Z_ROUNDS else dev(zl_, y, first, second, core)
+
+    def place(i, col):
+        first, second = (zh, x) if i in Z_ROUNDS else (x, zh)
+        u, v = (first + 4 - col) % 4, (second + 4 - col) % 4
+        p = (v + 3) % 4
+        return first, second, u % 2, u // 2, (u % 2 + u // 2) % 2, v, p
+
+    def stage(i, col, n):
+        first, second, j, s1, pq, v, p = place(i, col)
+        n = (n + 1) % 3 if i in Z_ROUNDS else n
+        if n == 0:
+            return s1, to_ring(i, (first + jnp.where(j == 1, 1, 3)) % 4, second, c)
+        if n == 1:
+            return p // 2, to_ring(i, first, (v + 1 - 2 * (v % 2) + col) % 4, c)
+        return p % 2, to_ring(i, first, (p + 2 - 2 * (p % 2) + col) % 4, c)
 
     def h_copy(i, col, d):
-        u, j, xh, pq = place(col)
-        q = (pq + d // 2) % 2 * 2 + (c + d % 2) % 2
-        xd, cd = quad_dst(col, q)
-        src = half_v.at[i, pl.ds(pl.multiple_of(col * 4 * hrows + q * hrows, 16), hrows)]
+        first, second, j, s1, pq, v, p = place(i, col)
+        q, cd = (pq + d // 2) % 2, (c + d % 2) % 2
+        fd = (s1 * 2 + (q + s1) % 2 + col) % 4
+        src = half_v.at[i, pl.ds(pl.multiple_of(col * 4 * hrows + (q * 2 + cd) * hrows, 16), hrows)]
         dst = quad_v.at[i, col, pl.ds(pl.multiple_of((j * 2 + c) * hrows, 16), hrows)]
         if d == 0:
             return pltpu.make_async_copy(src, dst, h_rsem.at[i, col])
-        return remote(src, dst, h_ssem, h_rsem.at[i, col], dev(zl, y, xd, zh, cd))
+        return remote(src, dst, h_ssem, h_rsem.at[i, col], to_ring(i, fd, second, cd))
 
     def half_step(i):
         df_copy(i).wait()
@@ -149,109 +159,95 @@
         copy.start()
     for i in range(1, ROUNDS):
         df_copy(i).start()
-    half_step(0)
-    half_send(0)
-    p_step()
-    half_step(1)
-    half_send(1, FIRST if 1 in LATE else FIRST + SECOND)
-
-    def p_last_step():
-        landed(pack_v.at[pl.ds(0, 3)], p_rsem.at[1])
-
-    p_last_step()
-
-    def w_step():
+
+    def w_step(i):
+        if i == 0:
+            landed(pack_v.at[pl.ds(0, 3)], p_rsem.at[1])
+            for copy in const_copies:
+                copy.wait()
         blocks = [
             [jnp.broadcast_to(pack_v[z][:, 16 * k : 16 * k + 1], (8, 128)) for k in range(8)] for z in range(4)
         ]
+        two = range(2)
         for col in range(2):
-            u, j, xh, pq = place(col)
-            wanted = jnp.concatenate(
-                [blocks[(z + 1 + col) % 4][(2 * h + jj + col) % 4 * 2 + cc] for h in range(2) for z in range(4) for jj in range(2) for cc in range(2)],
-                axis=0,
-            )
+            first, second, j, s1, pq, v, p = place(i, col)
+            if i in Z_ROUNDS:
+                order = [
+                    ((2 * h + jj + col) % 4, (2 * s2 + s3 + 1 + col) % 4, cc)
+                    for s2 in two for s3 in two for h in two for jj in two for cc in two
+                ]
+            else:
+                order = [
+                    ((2 * s2 + s3 + 1 + col) % 4, (2 * h + jj + col) % 4, cc)
+                    for h in two for s2 in two for s3 in two for jj in two for cc in two
+                ]
+            wanted = jnp.concatenate([blocks[z][xx * 2 + cc] for z, xx, cc in order], axis=0)
             at = lax.broadcasted_iota(jnp.int32, wanted.shape, 1)
             for n in range(natural // 128):
                 hot_v[:, n * 128 : (n + 1) * 128] = jnp.where(wanted == at + n * 128, 1.0, 0.0).astype(BF)
             total = None
-            for jj in range(2):
-                xs = (xh * 2 + jj + col) % 4
-                rows = rot_v[pl.ds(pl.multiple_of((xs * 4 + zh) * 80, 16), 80)]
-                sel = dot_nt(hot_v[...], rows).astype(BF)
+            for jj in two:
+                fs = (s1 * 2 + jj + col) % 4
+                chip = x * 4 + fs if i in Z_ROUNDS else fs * 4 + zh
+                sel = dot_nt(hot_v[...], rot_v[pl.ds(pl.multiple_of(chip * 80, 16), 80)]).astype(BF)
                 part = dot(sel, spread_v[jj])
                 total = part if total is None else total + part
-            w_v[col] = (total * mask_v[...].astype(F32)).astype(BF)
-
-    for copy in const_copies:
-        copy.wait()
-    w_step()
-
-    def zplace(col):
-        uz = (zh + 4 - col) % 4
-        return uz, (uz + 3) % 4
-
-    def x_partner(col):
-        return dev(zl, y, jnp.where(place(col)[1] == 1, xr, xl), zh, c)
-
-    def z_partner(col):
-        uz, p = zplace(col)
-        return dev(zl, y, x, (uz + 1 - 2 * (uz % 2) + col) % 4, c)
+            w_v[kind(i) * 2 + col] = (total * mask_v[...].astype(F32)).astype(BF)
+
+    def kind(i):
+        return 1 if i in Z_ROUNDS else 0
+
+    def half_rows(half, size):
+        return pl.ds(pl.multiple_of(half * size, size), size)
 
     def t_copy(i, col, n):
-        to = z_partner(col) if i in Z_FIRST else x_partner(col)
-        at = pl.ds(*pieces(i)[n])
-        return remote(tsend_v.at[i, col, :, at], trecv_v.at[i, col, :, at], t_ssem, t_rsem.at[i, col, n], to)
-
-    def w_rows(i, col, own):
-        xh, s = place(col)[2], zplace(col)[1] // 2
-        if i not in Z_FIRST:
-            return w_v[col, pl.ds(pl.multiple_of((xh if own else 1 - xh) * 128, 128), 128)]
-        s = s if own else 1 - s
-        return jnp.concatenate([w_v[col, pl.ds(pl.multiple_of((2 * h + s) * 64, 64), 64)] for h in range(2)], axis=0)
+        at = pl.ds(*pieces(i)[n])
+        return remote(
+            tsend_v.at[i, col, :, at], trecv_v.at[i, col, :, at], t_ssem, t_rsem.at[i, col, n], stage(i, col, 0)[1]
+        )
 
     def t_step(i, col, n):
         if n == 0:
             landed(quad_v.at[i, col], h_rsem.at[i, col])
         at = pl.ds(*pieces(i)[n])
-        tsend_v[i, col, :, at] = dot(w_rows(i, col, False), quad_v[i, col, :, at]).astype(BF)
+        half = stage(i, col, 0)[0]
+        w = w_v.at[kind(i) * 2 + col]
+        tsend_v[i, col, :, at] = dot(w[half_rows(1 - half, 128)], quad_v[i, col, :, at]).astype(BF)
         t_copy(i, col, n).start()
-        town_v[i, col, :, at] = dot(w_rows(i, col, True), quad_v[i, col, :, at])
+        town_v[i, col, :, at] = dot(w[half_rows(half, 128)], quad_v[i, col, :, at])
 
     def a_copy(i, col, n):
-        to = x_partner(col) if i in Z_FIRST else z_partner(col)
-        at = pl.ds(*pieces(i)[n])
-        return remote(asend_v.at[i, col, :, at], arecv_v.at[i, col, :, at], a_ssem, a_rsem.at[i, col, n], to)
+        at = pl.ds(*pieces(i)[n])
+        return remote(
+            asend_v.at[i, col, :, at], arecv_v.at[i, col, :, at], a_ssem, a_rsem.at[i, col, n], stage(i, col, 1)[1]
+        )
 
     def a_step(i, col, n):
         t_copy(i, col, n).wait_recv()
-        half = place(col)[2] if i in Z_FIRST else zplace(col)[1] // 2
-        at = pl.ds(*pieces(i)[n])
-        other = pl.ds(pl.multiple_of((1 - half) * 64, 64), 64)
-        own = pl.ds(pl.multiple_of(half * 64, 64), 64)
+        at = pl.ds(*pieces(i)[n])
+        half = stage(i, col, 1)[0]
+        other, own = half_rows(1 - half, 64), half_rows(half, 64)
         asend_v[i, col, :, at] = (town_v[i, col, other, at] + trecv_v[i, col, other, at].astype(F32)).astype(BF)
         a_copy(i, col, n).start()
         aown_v[i, col, :, at] = town_v[i, col, own, at] + trecv_v[i, col, own, at].astype(F32)
 
     def b_copy(i, col, n):
-        uz, p = zplace(col)
-        zd = (p + 2 - 2 * (p % 2) + col) % 4
         at = pl.ds(*pieces(i)[n])
         return remote(
-            bsend_v.at[i, col, :, at], brecv_v.at[i, col, :, at], b_ssem, b_rsem.at[i, col, n], dev(zl, y, x, zd, c)
+            bsend_v.at[i, col, :, at], brecv_v.at[i, col, :, at], b_ssem, b_rsem.at[i, col, n], stage(i, col, 2)[1]
         )
 
     def b_step(i, col, n):
         a_copy(i, col, n).wait_recv()
-        uz, p = zplace(col)
-        at = pl.ds(*pieces(i)[n])
-        other = pl.ds(pl.multiple_of((1 - p % 2) * 32, 32), 32)
-        own = pl.ds(pl.multiple_of(p % 2 * 32, 32), 32)
+        at = pl.ds(*pieces(i)[n])
+        half = stage(i, col, 2)[0]
+        other, own = half_rows(1 - half, 32), half_rows(half, 32)
         bsend_v[i, col, :, at] = (aown_v[i, col, other, at] + arecv_v[i, col, other, at].astype(F32)).astype(BF)
         b_copy(i, col, n).start()
         bown_v[i, col, :, at] = aown_v[i, col, own, at] + arecv_v[i, col, own, at].astype(F32)
 
     def g_copy(i, col, d):
-        u, j, xh, pq = place(col)
+        first, second, j, s1, pq, v, p = place(i, col)
         slot = (zl * 2 + j) * 2 + c
         to = (slot + d) % 8
         zd, jd, cd = to // 4, (to // 2) % 2, to % 2
@@ -259,7 +255,7 @@
         dst = gath_v.at[i * 2 + col, pl.ds(pl.multiple_of(slot * 16, 16), 16)]
         if d == 0:
             return pltpu.make_async_copy(src, dst, g_rsem.at[i, col])
-        return remote(src, dst, g_ssem, g_rsem.at[i, col], dev(zd, y, (xh * 2 + jd + col) % 4, zh, cd))
+        return remote(src, dst, g_ssem, g_rsem.at[i, col], to_ring(i, (s1 * 2 + jd + col) % 4, second, cd, zd))
 
     def f_step(i, col):
         for n in range(len(pieces(i))):
@@ -336,7 +332,6 @@
         landed(gath_v.at[pl.ds(0, 2 * ROUNDS - 1)], g_ssem)
 
     steps = {"t": t_step, "a": a_step, "b": b_step, "f": f_step, "y": y_step}
-    one_hots()
     for token in PLAN:
         name, i = token[0], int(token[1])
         if name == "h":
@@ -348,6 +343,12 @@
             out_step(i)
         elif name == "d":
             drain_step()
+        elif name == "p":
+            p_step()
+        elif name == "w":
+            w_step(i)
+        elif name == "c":
+            one_hots()
         elif name in "tab":
             for n in (int(token[2]),) if len(token) > 2 else range(len(pieces(i))):
                 for col in range(2):
@@ -419,7 +420,7 @@
                 vm((4, 8, 8, 128), jnp.int32),
                 vm((4, 8, 128), jnp.int32),
                 vm((256, nf), BF),
-                vm((2, 256, 4 * SUB * 40), BF),
+                vm((4, 256, 4 * SUB * 40), BF),
                 vm((ROUNDS, 2, 128, nf), BF),
                 vm((ROUNDS, 2, 128, nf), F32),
                 vm((ROUNDS, 2, 128, nf), BF),
@@ -441,9 +442,9 @@
                 dma(()),
                 dma((2,)), dma((2,)),
                 dma(()), dma((ROUNDS, 2)),
-                dma(()), dma((ROUNDS, 2, 2)),
-                dma(()), dma((ROUNDS, 2, 2)),
-                dma(()), dma((ROUNDS, 2, 2)),
+                dma(()), dma((ROUNDS, 2, 3)),
+                dma(()), dma((ROUNDS, 2, 3)),
+                dma(()), dma((ROUNDS, 2, 3)),
                 dma(()), dma((ROUNDS, 2)),
                 dma(()), dma((ROUNDS,)),
                 dma((2,)),

time: 74.8 us -> 69.9 us (0.934)
  Pallas kernels: 72.7 us -> 67.8 us
    pallas_call x1, Pallas kernels: 72.7 us -> 67.8 us  [local(): pl.pallas_call(kernel, name='tiles', out_shape=jax.ShapeDtypeStruct((80,...]
where the time goes in v3:
time: 69.9 us; the launch traced here: 69.7 us
  Pallas kernels  67.8 us (97%)
  local copies, waits for them, and re-layouts  1.97 us (3%)
    pallas_call x1, Pallas kernels, local(): pl.pallas_call(kernel, name='tiles', out_shape=jax.ShapeDtypeStruct((80,...  67.8 us
    reshape x1, local copies, waits for them, and re-layouts, local(): return out.reshape(80, 2, nf)  1.97 us

profile of v3, /device:TPU:1, one launch (start us, length us, event | category | flops | bytes accessed | tf_op | source)
XLA Modules:
  0.0 69.7 jit_solution(15936332229651333908)
XLA Ops:
  0.0 67.8 %tiles.1 = f32[80,1280]{1,0:T(8,128)} custom-call(bf16[2560,1280]{1,0:T(8,128)(2,1)} %bitcast.1, bf16[1280,640]{1,0:T(8,128)(2,1)} %rot_ref.1, s32[2,2]{1,0:T(2,128)} %pairs_ref.1, bf16[2,80,320]{2,1,0:T(8,128)(2,1)} %constant.4.clone.spread_ref, bf16[256,320]{1,0:T(8,128)(2,1)} %constant.5.clone.mask_ref), custom_call_target="tpu_custom_call" | custom-call | tf_op jit(solution)/shard_map/tiles/pallas_call | solution.py:401
  67.8 2.0 %reshape.7 = f32[80,2,640]{2,1,0:T(2,128)} reshape(f32[80,1280]{1,0:T(8,128)} %tiles.1) | data formatting | bytes 819200 | tf_op jit(solution)/shard_map/reshape | solution.py:462

commit v4 on v3

--- a/solution.py
+++ b/solution.py
@@ -16,14 +16,14 @@
 LATE = (2,)
 SPLIT = (0, 1, 2, 3)
 PLAN = (
-    "h0", "h3", "p0", "h1", "w0", "t0", "h2", "t3", "a0", "s2", "b0", "a3", "w1", "t2", "c0", "f0", "t1",
-    "b3", "a2", "f3", "y0", "a1", "b2", "b1", "y3", "f2", "f1", "o0", "y2", "o3", "y1", "o2", "d0", "o1",
+    "h3", "p0", "h1", "w0", "t0", "h2", "t3", "a0", "s2", "b0", "a3", "w1", "t2", "c0", "f0", "t1", "b3",
+    "a2", "f3", "y0", "a1", "b2", "b1", "y3", "f2", "f1", "o0", "y2", "o3", "y1", "o2", "d0", "o1",
 )
 SUB = 2
 
 
 def pieces(i):
-    return ((0, 384), (384, 256)) if i in SPLIT else ((0, 640),)
+    return ((0, 256), (256, 256), (512, 128)) if i in SPLIT else ((0, 640),)
 
 
 def dot(a, b):
@@ -39,7 +39,7 @@
     spread_v, mask_v, df_v, rot_v, half_v, quad_v, pair_v, pack_v, hot_v, w_v, tsend_v, town_v, trecv_v,
     asend_v, aown_v, arecv_v, bsend_v, bown_v, brecv_v, gsend_v, gath_v, order_v, pick_v, rows_v, ysend_v, acc_v,
     c_sem, df_sem, rot_sem, p_ssem, p_rsem, h_ssem, h_rsem, t_ssem, t_rsem,
-    a_ssem, a_rsem, b_ssem, b_rsem, g_ssem, g_rsem, y_ssem, y_rsem, o_sem,
+    a_ssem, a_rsem, b_ssem, b_rsem, g_ssem, g_rsem, y_ssem, y_rsem,
 ):
     natural = rot_v.shape[1]
     aux = lax.axis_index("aux")
@@ -120,7 +120,10 @@
 
     def half_step(i):
         df_copy(i).wait()
-        half_v[i] = dot(df_v[i], rot_v[...]).astype(BF)
+        for at in (pl.ds(0, rrows // 2), pl.ds(rrows // 2, rrows // 2)):
+            for lo in range(0, natural, 256):
+                to = pl.ds(lo, min(256, natural - lo))
+                half_v[i, at, to] = dot(df_v[i, at], rot_v[:, to]).astype(BF)
 
     def half_send(i, ds=(2, 3, 1, 0)):
         for d in ds:
@@ -147,9 +150,6 @@
         for d in (2, 1, 3):
             p_second(d).start()
 
-    pl.semaphore_wait(barrier, len(peers))
-    for n in range(7):
-        p_first(n).start()
     rot_copy.wait()
     const_copies = (
         pltpu.make_async_copy(spread_ref, spread_v, c_sem.at[0]),
@@ -159,6 +159,12 @@
         copy.start()
     for i in range(1, ROUNDS):
         df_copy(i).start()
+
+    half_step(0)
+    pl.semaphore_wait(barrier, len(peers))
+    for n in range(7):
+        p_first(n).start()
+    half_send(0)
 
     def w_step(i):
         if i == 0:
@@ -357,23 +363,8 @@
             for col in range(2):
                 steps[name](i, col)
 
-    def out_copy(t, n):
-        rows = 80 // 1
-        return pltpu.make_async_copy(
-            acc_v.at[pl.ds(128 * t + n * rows, rows)],
-            out_ref.at[pl.ds(n * rows, rows), pl.ds(natural * t, natural)],
-            o_sem.at[t],
-        )
-
-    def w_out_step():
-        for t in range(2):
-            for n in range(1):
-                out_copy(t, n).start()
-        for t in range(2):
-            for n in range(1):
-                out_copy(t, n).wait()
-
-    w_out_step()
+    for t in range(2):
+        out_ref[:, t, :] = acc_v[pl.ds(128 * t, 80)]
     landed(ysend_v, y_ssem)
 
 
@@ -398,10 +389,10 @@
         rows = aux_n * orbs // ROUNDS
         vm = pltpu.VMEM
         dma = pltpu.SemaphoreType.DMA
-        out = pl.pallas_call(
+        return pl.pallas_call(
             kernel,
             name="tiles",
-            out_shape=jax.ShapeDtypeStruct((80, 2 * nf), F32),
+            out_shape=pltpu.VMEM((80, 2, nf), F32),
             in_specs=[
                 pl.BlockSpec(memory_space=pl.ANY),
                 pl.BlockSpec(memory_space=pl.ANY),
@@ -409,7 +400,7 @@
                 pl.BlockSpec(memory_space=pl.ANY),
                 pl.BlockSpec(memory_space=pl.ANY),
             ],
-            out_specs=pl.BlockSpec(memory_space=pl.ANY),
+            out_specs=pl.BlockSpec(memory_space=pltpu.VMEM),
             scratch_shapes=[
                 vm((2, 80, 4 * SUB * 40), BF),
                 vm((256, 4 * SUB * 40), BF),
@@ -447,7 +438,6 @@
                 dma(()), dma((ROUNDS, 2, 3)),
                 dma(()), dma((ROUNDS, 2)),
                 dma(()), dma((ROUNDS,)),
-                dma((2,)),
             ],
             compiler_params=pltpu.CompilerParams(
                 collective_id=0, has_side_effects=True, vmem_limit_bytes=59392 * 2**10
@@ -459,7 +449,6 @@
             jnp.asarray(spread, BF),
             jnp.asarray(mask, BF),
         )
-        return out.reshape(80, 2, nf)
 
     placed = (P("aux", "virt", None), P(), P("virt", None))
     return jax.shard_map(local, mesh=mesh, in_specs=placed, out_specs=P("aux", "virt", None), check_vma=False)

time: 69.9 us -> 67.3 us (0.963)
  Pallas kernels: 67.8 us -> 66.4 us
  local copies, waits for them, and re-layouts: 1.97 us -> 0.75 us
    reshape x1 -> x0, local copies, waits for them, and re-layouts: 1.97 us -> none  [local(): return out.reshape(80, 2, nf)]
    pallas_call x1, Pallas kernels: 67.8 us -> 66.4 us  [local(): pl.pallas_call(kernel, name='tiles', out_shape=pltpu.VMEM((80, 2, nf), F3...]
    unnamed x0 -> x1, local copies, waits for them, and re-layouts: none -> 0.75 us
where the time goes in v4:
time: 67.3 us; the launch traced here: 67.2 us
  Pallas kernels  66.4 us (99%)
  local copies, waits for them, and re-layouts  0.75 us (1%)
    pallas_call x1, Pallas kernels, local(): pl.pallas_call(kernel, name='tiles', out_shape=pltpu.VMEM((80, 2, nf), F3...  66.4 us

profile of v4, /device:TPU:1, one launch (start us, length us, event | category | flops | bytes accessed | tf_op | source)
XLA Modules:
  0.0 67.2 jit_solution(8236002609425944283)
XLA Ops:
  0.0 66.4 %tiles.1 = f32[80,2,640]{2,1,0:T(2,128)S(1)} custom-call(bf16[2560,1280]{1,0:T(8,128)(2,1)} %bitcast.1, bf16[1280,640]{1,0:T(8,128)(2,1)} %rot_ref.1, s32[2,2]{1,0:T(2,128)} %pairs_ref.1, bf16[2,80,320]{2,1,0:T(8,128)(2,1)} %constant.4.clone.spread_ref, bf16[256,320]{1,0:T(8,128)(2,1)} %constant.5.clone.mask_ref), custom_call_target="tpu_custom_call" | custom-call | tf_op jit(solution)/shard_map/tiles/pallas_call | solution.py:392
  66.4 0.8 %copy.7 = f32[80,2,640]{2,1,0:T(2,128)} copy(f32[80,2,640]{2,1,0:T(2,128)S(1)} %tiles.1) | data formatting | bytes 819200

commit v5 on v4

--- a/solution.py
+++ b/solution.py
@@ -23,7 +23,7 @@
 
 
 def pieces(i):
-    return ((0, 256), (256, 256), (512, 128)) if i in SPLIT else ((0, 640),)
+    return ((0, 384), (384, 256)) if i in SPLIT else ((0, 640),)
 
 
 def dot(a, b):
@@ -63,9 +63,14 @@
     def df_copy(i):
         return pltpu.make_async_copy(df_ref.at[pl.ds(i * rrows, rrows)], df_v.at[i], df_sem.at[i])
 
-    rot_copy = pltpu.make_async_copy(rot_ref, rot_v, rot_sem)
-    rot_copy.start()
-    df_copy(0).start()
+    first_copies = []
+    for n in range(4):
+        at = pl.ds(n * rot_v.shape[0] // 4, rot_v.shape[0] // 4)
+        first_copies.append(pltpu.make_async_copy(rot_ref.at[at], rot_v.at[at], rot_sem))
+        at = pl.ds(n * rrows // 4, rrows // 4)
+        first_copies.append(pltpu.make_async_copy(df_ref.at[at], df_v.at[0, at], df_sem.at[0]))
+    for copy in first_copies:
+        copy.start()
 
     xr, xl = (x + 1) % 4, (x + 3) % 4
     xo = (x + 2) % 4
@@ -119,7 +124,7 @@
         return remote(src, dst, h_ssem, h_rsem.at[i, col], to_ring(i, fd, second, cd))
 
     def half_step(i):
-        df_copy(i).wait()
+        landed(df_v.at[i], df_sem.at[i])
         for at in (pl.ds(0, rrows // 2), pl.ds(rrows // 2, rrows // 2)):
             for lo in range(0, natural, 256):
                 to = pl.ds(lo, min(256, natural - lo))
@@ -150,17 +155,16 @@
         for d in (2, 1, 3):
             p_second(d).start()
 
-    rot_copy.wait()
+    landed(rot_v, rot_sem)
     const_copies = (
         pltpu.make_async_copy(spread_ref, spread_v, c_sem.at[0]),
         pltpu.make_async_copy(mask_ref, mask_v, c_sem.at[1]),
     )
+    half_step(0)
+    for i in (3, 1, 2):
+        df_copy(i).start()
     for copy in const_copies:
         copy.start()
-    for i in range(1, ROUNDS):
-        df_copy(i).start()
-
-    half_step(0)
     pl.semaphore_wait(barrier, len(peers))
     for n in range(7):
         p_first(n).start()
@@ -191,13 +195,13 @@
             at = lax.broadcasted_iota(jnp.int32, wanted.shape, 1)
             for n in range(natural // 128):
                 hot_v[:, n * 128 : (n + 1) * 128] = jnp.where(wanted == at + n * 128, 1.0, 0.0).astype(BF)
-            total = None
+            rows = []
             for jj in two:
                 fs = (s1 * 2 + jj + col) % 4
                 chip = x * 4 + fs if i in Z_ROUNDS else fs * 4 + zh
-                sel = dot_nt(hot_v[...], rot_v[pl.ds(pl.multiple_of(chip * 80, 16), 80)]).astype(BF)
-                part = dot(sel, spread_v[jj])
-                total = part if total is None else total + part
+                rows.append(rot_v[pl.ds(pl.multiple_of(chip * 80, 16), 80)])
+            sel = dot_nt(hot_v[...], jnp.concatenate(rows, axis=0)).astype(BF)
+            total = dot(sel, spread_v[...].reshape(160, 4 * SUB * 40))
             w_v[kind(i) * 2 + col] = (total * mask_v[...].astype(F32)).astype(BF)
 
     def kind(i):
@@ -220,7 +224,10 @@
         w = w_v.at[kind(i) * 2 + col]
         tsend_v[i, col, :, at] = dot(w[half_rows(1 - half, 128)], quad_v[i, col, :, at]).astype(BF)
         t_copy(i, col, n).start()
-        town_v[i, col, :, at] = dot(w[half_rows(half, 128)], quad_v[i, col, :, at])
+
+    def t_own_step(i, col):
+        w = w_v.at[kind(i) * 2 + col]
+        town_v[i, col] = dot(w[half_rows(stage(i, col, 0)[0], 128)], quad_v[i, col])
 
     def a_copy(i, col, n):
         at = pl.ds(*pieces(i)[n])
@@ -255,8 +262,7 @@
     def g_copy(i, col, d):
         first, second, j, s1, pq, v, p = place(i, col)
         slot = (zl * 2 + j) * 2 + c
-        to = (slot + d) % 8
-        zd, jd, cd = to // 4, (to // 2) % 2, to % 2
+        zd, jd, cd = (zl + d // 4) % 2, (j + d // 2) % 2, (c + d) % 2
         src = gsend_v.at[i, col, zd, pl.ds(pl.multiple_of((jd * 2 + cd) * 16, 16), 16)]
         dst = gath_v.at[i * 2 + col, pl.ds(pl.multiple_of(slot * 16, 16), 16)]
         if d == 0:
@@ -275,7 +281,7 @@
             upper = jnp.concatenate([win[0], win[1]], axis=1).reshape(4, 8, 256)
             under = jnp.concatenate([win[2], shared], axis=1).reshape(4, 8, 256)
             gsend_v[i, col, w] = jnp.concatenate([upper, under], axis=1).reshape(64, 256).astype(BF)
-        for d in (4, 5, 6, 7, 2, 3, 1, 0):
+        for d in (7, 6, 5, 4, 3, 2, 1, 0):
             g_copy(i, col, d).start()
 
     def y_copy(i, col, d):
@@ -359,6 +365,9 @@
             for n in (int(token[2]),) if len(token) > 2 else range(len(pieces(i))):
                 for col in range(2):
                     steps[name](i, col, n)
+            if name == "t":
+                for col in range(2):
+                    t_own_step(i, col)
         else:
             for col in range(2):
                 steps[name](i, col)

time: 67.3 us -> 67 us (level)
  no operation moved by 1% of the time
where the time goes in v5:
time: 67 us; the launch traced here: 66.9 us
  Pallas kernels  66.1 us (99%)
  local copies, waits for them, and re-layouts  0.75 us (1%)
    pallas_call x1, Pallas kernels, local(): pl.pallas_call(kernel, name='tiles', out_shape=pltpu.VMEM((80, 2, nf), F3...  66.1 us

profile of v5, /device:TPU:1, one launch (start us, length us, event | category | flops | bytes accessed | tf_op | source)
XLA Modules:
  0.0 66.9 jit_solution(10818630271839753156)
XLA Ops:
  0.0 66.1 %tiles.1 = f32[80,2,640]{2,1,0:T(2,128)S(1)} custom-call(bf16[2560,1280]{1,0:T(8,128)(2,1)} %bitcast.1, bf16[1280,640]{1,0:T(8,128)(2,1)} %rot_ref.1, s32[2,2]{1,0:T(2,128)} %pairs_ref.1, bf16[2,80,320]{2,1,0:T(8,128)(2,1)} %constant.4.clone.spread_ref, bf16[256,320]{1,0:T(8,128)(2,1)} %constant.5.clone.mask_ref), custom_call_target="tpu_custom_call" | custom-call | tf_op jit(solution)/shard_map/tiles/pallas_call | solution.py:401
  66.1 0.8 %copy.7 = f32[80,2,640]{2,1,0:T(2,128)} copy(f32[80,2,640]{2,1,0:T(2,128)S(1)} %tiles.1) | data formatting | bytes 819200

commit v6 on v5

--- a/solution.py
+++ b/solution.py
@@ -311,16 +311,21 @@
                 rows_v[y, i, col, :, :natural] = right
                 rows_v[y, i, col, :, natural:] = left
 
-    def out_step(i):
+    def out_step(i, last):
         landed(rows_v.at[pl.ds(0, 3), i], y_rsem.at[i])
         both = rows_v[:, i].reshape(256, natural + 128)
         left = both[:, natural:]
         parity = lax.broadcasted_iota(jnp.int32, left.shape, 0) % 2
         zero = jnp.zeros_like(left)
         left = jnp.concatenate([jnp.where(parity == t, left, zero) for t in range(2)], axis=1)
-        acc_v[...] += lax.dot_general(
+        total = acc_v[...] + lax.dot_general(
             left, both[:, :natural], (((0,), (0,)), ((), ())), preferred_element_type=F32
         )
+        if last:
+            for t in range(2):
+                out_ref[:, t, :] = total[128 * t : 128 * t + 80]
+        else:
+            acc_v[...] = total
 
     def one_hots():
         to = lax.broadcasted_iota(jnp.int32, (64, 128), 0)
@@ -352,7 +357,7 @@
         elif name == "s":
             half_send(i, SECOND)
         elif name == "o":
-            out_step(i)
+            out_step(i, token == PLAN[-1])
         elif name == "d":
             drain_step()
         elif name == "p":
@@ -372,8 +377,6 @@
             for col in range(2):
                 steps[name](i, col)
 
-    for t in range(2):
-        out_ref[:, t, :] = acc_v[pl.ds(128 * t, 80)]
     landed(ysend_v, y_ssem)
 
 

time: 67 us -> 67 us (level)
  no operation moved by 1% of the time
where the time goes in v6:
time: 67 us; the launch traced here: 66.9 us
  Pallas kernels  66.1 us (99%)
  local copies, waits for them, and re-layouts  0.75 us (1%)
    pallas_call x1, Pallas kernels, local(): pl.pallas_call(kernel, name='tiles', out_shape=pltpu.VMEM((80, 2, nf), F3...  66.1 us

profile of v6, /device:TPU:1, one launch (start us, length us, event | category | flops | bytes accessed | tf_op | source)
XLA Modules:
  0.0 66.9 jit_solution(10917954002403872660)
XLA Ops:
  0.0 66.1 %tiles.1 = f32[80,2,640]{2,1,0:T(2,128)S(1)} custom-call(bf16[2560,1280]{1,0:T(8,128)(2,1)} %bitcast.1, bf16[1280,640]{1,0:T(8,128)(2,1)} %rot_ref.1, s32[2,2]{1,0:T(2,128)} %pairs_ref.1, bf16[2,80,320]{2,1,0:T(8,128)(2,1)} %constant.4.clone.spread_ref, bf16[256,320]{1,0:T(8,128)(2,1)} %constant.5.clone.mask_ref), custom_call_target="tpu_custom_call" | custom-call | tf_op jit(solution)/shard_map/tiles/pallas_call | solution.py:404
  66.1 0.8 %copy.7 = f32[80,2,640]{2,1,0:T(2,128)} copy(f32[80,2,640]{2,1,0:T(2,128)S(1)} %tiles.1) | data formatting | bytes 819200
